TPU v7x, 256 devices: a whole 4x4x8 slice. The times are simulated.
256 devices in a mesh: cuts: 2 (over x_hi), fsdp: 32 (over z, y), tp: 4 (over x_lo, core).
Axes of the slice: x: 4 (x_hi: 2, x_lo: 2; x = x_hi * 2 + x_lo), y: 4, z: 8, core: 2. Of those that a mesh axis runs over, the one named last changes fastest.
Arguments:
- hidden: bfloat16 [10240, 14336], P(('cuts', 'fsdp'), 'tp'), may hold values from -6 to 6
- grad_out: bfloat16 [10240, 4096], P(('cuts', 'fsdp'), 'tp'), may hold values from -16 to 16
- weight: bfloat16 [2, 4096, 14336], P('cuts', 'fsdp', 'tp'), may hold values from -6 to 6
- anchor: float32 [4096, 14336], P('fsdp', 'tp'), may hold values from -6 to 6
- momentum: float32 [4096, 14336], P('fsdp', 'tp'), may hold values from -3 to 3
Outputs:
- grad_hidden: bfloat16 [10240, 14336], P(('cuts', 'fsdp'), 'tp')
- mixed: bfloat16 [2, 4096, 14336], P('cuts', 'fsdp', 'tp')
- new_anchor: float32 [4096, 14336], P('fsdp', 'tp')
- new_momentum: float32 [4096, 14336], P('fsdp', 'tp')
All inputs are finite; a program needn't handle non-finite values.
Results may differ from a plain program's by a relative error of at most 0.024.
Values may be sent and summed in bfloat16 or wider, within the bound.
No kernel may reach another device: no remote copies, remote signals or barrier semaphores. Data moves between devices by JAX's collectives and lax.ppermute only.
A program may use at most 192 MiB of HBM per device.

v0:
```python
import jax
import jax.numpy as jnp
from jax import lax
from jax.sharding import Mesh
from jax.sharding import PartitionSpec as P

inner_rate = 1.0
outer_rate = 0.7
momentum_decay = 0.9
mix_weight = 0.5

Z, Y = 8, 4
f32, bf16 = jnp.float32, jnp.bfloat16
tie = lax.optimization_barrier


def shift(x, axis, by):
    n = lax.axis_size(axis)
    return lax.ppermute(x, axis, [(i, (i + by) % n) for i in range(n)])


def cross(x, by):
    perm = [(c * Y + i, (1 - c) * Y + (i + by) % Y) for c in range(2) for i in range(Y)]
    return lax.ppermute(x, ("cuts", "y"), perm)


def local(hidden, grad_out, weight, anchor, momentum):
    width = hidden.shape[1]
    factor = (width * 4) ** (-0.5)
    z, y = lax.axis_index("z"), lax.axis_index("y")
    t = lax.axis_index("xl") * 2 + lax.axis_index("core")
    part = width // Y
    rows = weight.shape[1]
    deep = rows * Y
    toks = hidden.shape[0]
    local_w = weight[0]
    half = deep // 2

    def columns(x, k):
        return lax.dynamic_slice_in_dim(x, k % Y * part, part, axis=1)

    def band(x, k):
        return lax.dynamic_slice_in_dim(x, k % Y * rows, rows, axis=0)

    g_all = lax.all_gather(grad_out, ("y", "xl", "core")).reshape(Y, -1, toks, grad_out.shape[1])
    per = grad_out.shape[1] // deep

    def features(k):
        k = k % Z
        at, size = (0, k // per, 0, k % per * deep), (Y, 1, toks, deep)
        return lax.dynamic_slice(g_all, at, size).reshape(Y * toks, deep)

    def gathered(x):
        parts = {d: shift(columns(x, y + d), "y", d) for d in (2, 1, 3)}
        parts[0] = columns(x, y)
        n = x.shape[0]
        whole = jnp.zeros((Y * n, part), bf16)
        for d in (0, 1, 3, 2):
            whole = lax.dynamic_update_slice_in_dim(whole, parts[d], (y - d) % Y * n, axis=0)
        return whole

    w_mine = gathered(local_w)
    h_sent = jnp.stack([hidden[:, k * part : (k + 1) * part] for k in range(Y)])
    h_mine = lax.all_to_all(h_sent, "y", 0, 0, tiled=True).reshape(Y * toks, part)

    ups, downs = [w_mine], [w_mine]
    for k in (1, 2):
        ups.append(shift(ups[-1], "z", 1))
        downs.append(shift(downs[-1], "z", -1))
    ups[2], downs[2], h_mine = tie((ups[2], downs[2], h_mine))
    ups.append(shift(ups[2], "z", 1))
    downs.append(shift(downs[2], "z", -1))

    def term(k):
        return factor * lax.dot_general(
            features(k), h_mine, (((0,), (0,)), ((), ())), preferred_element_type=f32
        )

    def product(k, w_block):
        return jnp.dot(features(k), w_block, preferred_element_type=f32)

    far = term(z + 4).astype(bf16)
    up, down = shift(far[:half], "z", 1), shift(far[half:], "z", -1)
    up, down, ups[3], downs[3] = tie((up, down, ups[3], downs[3]))
    b = term(z + 3)
    up = jnp.concatenate([b[:half] + up.astype(f32), b[half:]], axis=0)
    b = term(z - 3)
    down = jnp.concatenate([b[:half], b[half:] + down.astype(f32)], axis=0)
    up, down = shift(up.astype(bf16), "z", 1), shift(down.astype(bf16), "z", -1)
    last = [shift(ups[3][:half], "z", 1), shift(downs[3][half:], "z", -1)]
    total = product(z, w_mine)
    for k in (1, 2, 3):
        total = total + product(z - k, ups[k]) + product(z + k, downs[k])
    up, down, total, last = tie((up, down, total, last))
    up = (term(z + 2) + up.astype(f32)).astype(bf16)
    down = (term(z - 2) + down.astype(f32)).astype(bf16)
    up, down = shift(up, "z", 1), shift(down, "z", -1)

    total = total + product(z + 4, jnp.concatenate(last, axis=0))
    grad_h = (factor * total).astype(bf16)
    back = lax.all_to_all(grad_h.reshape(Y, toks, part), "y", 0, 0, tiled=True)
    up, down, back = tie((up, down, back))
    grad_hidden = jnp.concatenate([back[k] for k in range(Y)], axis=1)

    up = (term(z + 1) + up.astype(f32)).astype(bf16)
    down = (term(z - 1) + down.astype(f32)).astype(bf16)
    up, down = shift(up, "z", 1), shift(down, "z", -1)
    grad_w = term(z) + up.astype(f32) + down.astype(f32)
    inner_t = (w_mine.astype(f32) - inner_rate * grad_w).astype(bf16)

    sent = jnp.concatenate([inner_t, inner_t], axis=0).reshape(2 * Y, rows, part)
    got = lax.all_to_all(sent, ("cuts", "y"), 0, 0, tiled=True)
    c = lax.axis_index("cuts")

    def of(c):
        blocks = lax.dynamic_slice_in_dim(got, c * Y, Y, axis=0)
        return jnp.concatenate([blocks[k] for k in range(Y)], axis=1)

    inner, other = of(c), of(1 - c)

    def delta(x):
        return (anchor - x.astype(f32)).astype(bf16).astype(f32)

    average = (delta(inner) + delta(other)) / lax.axis_size("cuts")
    new_momentum = momentum_decay * momentum + average
    new_anchor = anchor - outer_rate * (average + momentum_decay * new_momentum)
    mixed = (mix_weight * inner.astype(f32) + (1.0 - mix_weight) * new_anchor).astype(bf16)

    return (grad_hidden, mixed[None], new_anchor, new_momentum)


def solution(mesh):
    grid = Mesh(mesh.devices.reshape(2, Z, Y, 2, 2), ("cuts", "z", "y", "xl", "core"))
    tokens, rows, units = P(("cuts", "z", "y"), ("xl", "core")), ("z", "y"), ("xl", "core")
    return jax.shard_map(
        local,
        mesh=grid,
        in_specs=(tokens, tokens, P("cuts", rows, units), P(rows, units), P(rows, units)),
        out_specs=(tokens, P("cuts", rows, units), P(rows, units), P(rows, units)),
        check_vma=False,
    )
```

profile of v0, /device:TPU:6, one launch (start us, length us, event | category | flops | bytes accessed | tf_op | source)
XLA Modules:
  0.0 211.1 jit_solution(4028550309418594066)
XLA Ops:
  8.0 1.3 dynamic-slice_bitcast_fusion.8
  9.3 1.7 collective-permute-start
  10.9 1.7 collective-permute-start.1
  12.6 2.0 collective-permute-start.2
  15.6 2.3 %collective-permute-done = bf16[128,896]{1,0:T(8,128)(2,1)S(1)} collective-permute-done((bf16[128,896]{1,0:T(8,128)(2,1)S(1)}, bf16[128,896]{1,0:T(8,128)(2,1)S(1)}, u32[]{:S(2)}, u32[]{:S(2)}) %collective-permute-start) | collective-permute-done | bytes 229408 | tf_op jit(solution)/shard_map/ppermute | solution.py:19
  18.0 4.3 %collective-permute-done.1 = bf16[128,896]{1,0:T(8,128)(2,1)S(1)} collective-permute-done((bf16[128,896]{1,0:T(8,128)(2,1)S(1)}, bf16[128,896]{1,0:T(8,128)(2,1)S(1)}, u32[]{:S(2)}, u32[]{:S(2)}) %collective-permute-start.1) | collective-permute-done | bytes 229408 | tf_op jit(solution)/shard_map/ppermute | solution.py:19
  22.3 1.8 collective-permute-done.2
  24.1 2.0 collective-permute-start.3
  26.1 4.0 %collective-permute-start.5 = (bf16[512,896]{1,0:T(8,128)(2,1)S(1)}, bf16[512,896]{1,0:T(8,128)(2,1)S(1)}, u32[]{:S(2)}, u32[]{:S(2)}) collective-permute-start(bf16[512,896]{1,0:T(8,128)(2,1)S(1)} %constant_dynamic-update-slice_fusion), channel_id=1, source_target_pairs={{0,112},{16,0},{32,16},{48,32},{64,48},{80,64},{96,80},{112,96},{1... | collective-permute-start | bytes 2752520 | tf_op jit(solution)/shard_map/ppermute | solution.py:19
  30.2 19.4 %collective-permute-done.3 = bf16[512,896]{1,0:T(8,128)(2,1)} collective-permute-done((bf16[512,896]{1,0:T(8,128)(2,1)S(1)}, bf16[512,896]{1,0:T(8,128)(2,1)}, u32[]{:S(2)}, u32[]{:S(2)}) %collective-permute-start.3) | collective-permute-done | bytes 917536 | tf_op jit(solution)/shard_map/ppermute | solution.py:19
  49.6 3.2 %collective-permute-start.6 = (bf16[512,896]{1,0:T(8,128)(2,1)S(1)}, bf16[512,896]{1,0:T(8,128)(2,1)}, u32[]{:S(2)}, u32[]{:S(2)}) collective-permute-start(bf16[512,896]{1,0:T(8,128)(2,1)S(1)} %collective-permute-done.5), channel_id=1, source_target_pairs={{0,112},{16,0},{32,16},{48,32},{64,48},{80,64},{96,80},{112,96},{1... | collective-permute-start | bytes 2752520 | tf_op jit(solution)/shard_map/ppermute | solution.py:19
  52.9 1.2 pad_maximum_fusion.1
  54.0 3.5 %all-to-all-start = ((bf16[4,160,896]{2,1,0:T(8,128)(2,1)}), bf16[4,160,896]{2,1,0:T(8,128)(2,1)S(1)}, u32[]{:S(2)}, u32[]{:S(2)}) async-start(bf16[4,160,896]{2,1,0:T(8,128)(2,1)} %pad_maximum_fusion.1), calls=%async_computation | async-start | bytes 2293760 | tf_op jit(solution)/shard_map/all_to_all | solution.py:64
  58.0 13.9 %all-to-all-done = bf16[4,160,896]{2,1,0:T(8,128)(2,1)S(1)} async-done(((bf16[4,160,896]{2,1,0:T(8,128)(2,1)}), bf16[4,160,896]{2,1,0:T(8,128)(2,1)S(1)}, u32[]{:S(2)}, u32[]{:S(2)}) %all-to-all-start) | async-done | bytes 1146912 | tf_op jit(solution)/shard_map/all_to_all | solution.py:64
  71.9 1.0 copy-done.3
  72.9 1.6 collective-permute-start.10
  74.9 3.1 %constant_dynamic-slice_fusion.2 = (bf16[4,1,160,512]{3,2,1,0:T(8,128)(2,1)S(1)}, bf16[4,1,160,512]{3,2,1,0:T(8,128)(2,1)S(1)}, bf16[4,1,160,512]{3,2,1,0:T(8,12...) fusion(bf16[4,4,160,1024]{3,2,1,0:T(8,128)(2,1)} %bitcast.86, ...), kind=kLoop, calls=%fused_computation.58 | loop fusion | bytes 10485824 | tf_op jit(solution)/shard_map/dynamic_slice | solution.py:51
  78.1 1.0 multiply_convert_fusion.1
  79.2 3.2 %collective-permute-start.8 = (bf16[256,896]{1,0:T(8,128)(2,1)S(1)}, bf16[256,896]{1,0:T(8,128)(2,1)S(1)}, u32[]{:S(2)}, u32[]{:S(2)}) collective-permute-start(bf16[256,896]{1,0:T(8,128)(2,1)S(1)} %get-tuple-element.61), channel_id=1, source_target_pairs={{0,112},{16,0},{32,16},{48,32},{64,48},{80,64},{96,80},{112,96},{1... | collective-permute-start | bytes 1376264 | tf_op jit(solution)/shard_map/ppermute | solution.py:19
  82.5 2.0 fusion.15
  85.3 2.0 fusion.13
  87.4 1.0 convolution_multiply_fusion
  88.3 1.0 convolution_multiply_fusion.1
  89.5 1.1 copy-done.6
  91.4 5.0 %collective-permute-done.10 = bf16[512,896]{1,0:T(8,128)(2,1)S(1)} collective-permute-done((bf16[512,896]{1,0:T(8,128)(2,1)}, bf16[512,896]{1,0:T(8,128)(2,1)S(1)}, u32[]{:S(2)}, u32[]{:S(2)}) %collective-permute-start.10) | collective-permute-done | bytes 917536 | tf_op jit(solution)/shard_map/ppermute | solution.py:19
  96.4 2.8 %collective-permute-done.9 = bf16[512,896]{1,0:T(8,128)(2,1)S(1)} collective-permute-done((bf16[512,896]{1,0:T(8,128)(2,1)}, bf16[512,896]{1,0:T(8,128)(2,1)S(1)}, u32[]{:S(2)}, u32[]{:S(2)}) %collective-permute-start.9) | collective-permute-done | bytes 917536 | tf_op jit(solution)/shard_map/ppermute | solution.py:19
  99.2 5.6 %collective-permute-done.7 = bf16[256,896]{1,0:T(8,128)(2,1)S(1)} collective-permute-done((bf16[256,896]{1,0:T(8,128)(2,1)S(1)}, bf16[256,896]{1,0:T(8,128)(2,1)S(1)}, u32[]{:S(2)}, u32[]{:S(2)}) %collective-permute-start.7) | collective-permute-done | bytes 458784 | tf_op jit(solution)/shard_map/ppermute | solution.py:19
  106.4 1.8 collective-permute-start.11
  108.4 3.2 %collective-permute-start.14 = (bf16[256,896]{1,0:T(8,128)(2,1)S(1)}, bf16[256,896]{1,0:T(8,128)(2,1)S(1)}, u32[]{:S(2)}, u32[]{:S(2)}) collective-permute-start(bf16[256,896]{1,0:T(8,128)(2,1)S(1)} %slice.85), channel_id=1, source_target_pairs={{0,112},{16,0},{32,16},{48,32},{64,48},{80,64},{96,80},{112,96},{1... | collective-permute-start | bytes 1376264 | tf_op jit(solution)/shard_map/ppermute | solution.py:19
  112.4 2.3 %add_add_fusion = f32[640,896]{1,0:T(8,128)S(1)} fusion(f32[640,896]{1,0:T(8,128)S(1)} %fusion.17, f32[640,896]{1,0:T(8,128)S(1)} %fusion.16, f32[640,896]{1,0:T(8,128)S(1)} %fusion.15, f32[640,896]{1,0:T(8,128)S(1)} %fusion.14, f32[640,896]{1,0:T(8,128)S(1)} %fusion.12, f32[640,896]{1,0:T(8,128)S(1)} %fusion.13, bf16[640,512]{1,0:T(8,128)(2,1)S(1)} %bitcast.90, ...), kind=kOutput, calls=%fused_computation.1 | convolution fusion | flops 590643200 | bytes 17629184 | tf_op jit(solution)/shard_map/dot_general | solution.py:80
  114.7 21.0 %collective-permute-done.13 = bf16[256,896]{1,0:T(8,128)(2,1)S(1)} collective-permute-done((bf16[256,896]{1,0:T(8,128)(2,1)S(1)}, bf16[256,896]{1,0:T(8,128)(2,1)S(1)}, u32[]{:S(2)}, u32[]{:S(2)}) %collective-permute-start.13) | collective-permute-done | bytes 458784 | tf_op jit(solution)/shard_map/ppermute | solution.py:19
  135.7 1.0 add_convert_fusion.2
  136.8 1.0 add_convert_fusion.3
  137.8 2.3 %collective-permute-start.15 = (bf16[512,896]{1,0:T(8,128)(2,1)S(1)}, bf16[512,896]{1,0:T(8,128)(2,1)S(1)}, u32[]{:S(2)}, u32[]{:S(2)}) collective-permute-start(bf16[512,896]{1,0:T(8,128)(2,1)S(1)} %add_convert_fusion.3), channel_id=1, source_target_pairs={{0,16},{16,32},{32,48},{48,64},{64,80},{80,96},{96,112},{112,0},{1... | collective-permute-start | bytes 2752520 | tf_op jit(solution)/shard_map/ppermute | solution.py:19
  141.3 14.6 %all_to_all.15 = bf16[4,160,896]{2,1,0:T(8,128)(2,1)} all-to-all(bf16[4,160,896]{2,1,0:T(8,128)(2,1)S(1)} %bitcast.87), channel_id=1, replica_groups=mesh['cuts'=2,'z'=8,'y'=4,'xl'=2,'core'=2] {'y'}, dimensions={0} | all-to-all | bytes 2293760 | tf_op jit(solution)/shard_map/all_to_all | solution.py:101
  155.8 1.6 collective-permute-done.15
  157.4 1.0 add_convert_fusion.1
  158.4 2.0 collective-permute-start.17
  160.4 1.0 add_convert_fusion
  161.4 1.4 collective-permute-start.18
  163.8 12.4 %collective-permute-done.17 = bf16[512,896]{1,0:T(8,128)(2,1)S(1)} collective-permute-done((bf16[512,896]{1,0:T(8,128)(2,1)S(1)}, bf16[512,896]{1,0:T(8,128)(2,1)S(1)}, u32[]{:S(2)}, u32[]{:S(2)}) %collective-permute-start.17) | collective-permute-done | bytes 917536 | tf_op jit(solution)/shard_map/ppermute | solution.py:19
  176.7 1.4 pad_maximum_fusion
  178.1 4.9 %all-to-all-start.2 = ((bf16[8,128,896]{2,1,0:T(8,128)(2,1)}), bf16[8,128,896]{2,1,0:T(8,128)(2,1)S(1)}, u32[]{:S(2)}, u32[]{:S(2)}) async-start(bf16[8,128,896]{2,1,0:T(8,128)(2,1)} %bitcast.85), calls=%async_computation.2 | async-start | bytes 3670016 | tf_op jit(solution)/shard_map/all_to_all | solution.py:112
  183.0 1.3 slice_bitcast_fusion.3
  184.3 1.1 pad_maximum_fusion.2
  185.4 14.1 %all-to-all-done.2 = bf16[8,128,896]{2,1,0:T(8,128)(2,1)S(1)} async-done(((bf16[8,128,896]{2,1,0:T(8,128)(2,1)}), bf16[8,128,896]{2,1,0:T(8,128)(2,1)S(1)}, u32[]{:S(2)}, u32[]{:S(2)}) %all-to-all-start.2) | async-done | bytes 1835040 | tf_op jit(solution)/shard_map/all_to_all | solution.py:112
  199.6 1.3 copy-done
  201.5 2.7 %fusion.3 = (bf16[1,128,3584]{2,1,0:T(8,128)(2,1)}, f32[128,3584]{1,0:T(8,128)}, f32[128,3584]{1,0:T(8,128)}) fusion(bf16[128,896]{1,0:T(8,128)(2,1)S(1)} %get-tuple-element.52, bf16[128,896]{1,0:T(8,128)(2,1)S(1)} %get-tuple-element.48, bf16[128,896]{1,0:T(8,128)(2,1)S(1)} %get-tuple-element.49, bf16[128,896]{1,0:T(8,128)(2,1)S(1)} %get-tuple-element.50, ...), kind=kLoop, calls=%fused_computation.22 | loop fusion | flops 15138816 | bytes 10092544 | tf_op jit(solution)/shard_map/broadcast_in_dim | solution.py:129
  (53 shorter events, 10.3 us)
Async XLA Ops:
  7.2 67.7 %all-gather.3.cloned.1.call-start = ((), (), s32[]{:S(2)}) async-start(), calls=%async_computation.3 | async-start | bytes 5570560 | tf_op jit(solution)/shard_map/all_gather | solution.py:45
  7.9 22.2 %copy-start.2 = (bf16[160,3584]{1,0:T(8,128)(2,1)S(1)}, bf16[160,3584]{1,0:T(8,128)(2,1)}, u32[]{:S(2)}) copy-start(bf16[160,3584]{1,0:T(8,128)(2,1)} %param.5) | copy-start | bytes 3440644
  9.3 8.7 %collective-permute-start = (bf16[128,896]{1,0:T(8,128)(2,1)S(1)}, bf16[128,896]{1,0:T(8,128)(2,1)S(1)}, u32[]{:S(2)}, u32[]{:S(2)}) collective-permute-start(bf16[128,896]{1,0:T(8,128)(2,1)S(1)} %get-tuple-element.64), channel_id=1, source_target_pairs={{0,4},{4,8},{8,12},{12,0},{1,5},{5,9},{9,13},{13,1},{2,6},{6,10},{... | collective-permute-start | bytes 688136 | tf_op jit(solution)/shard_map/ppermute | solution.py:19
  10.9 11.3 %collective-permute-start.1 = (bf16[128,896]{1,0:T(8,128)(2,1)S(1)}, bf16[128,896]{1,0:T(8,128)(2,1)S(1)}, u32[]{:S(2)}, u32[]{:S(2)}) collective-permute-start(bf16[128,896]{1,0:T(8,128)(2,1)S(1)} %get-tuple-element.65), channel_id=1, source_target_pairs={{0,12},{4,0},{8,4},{12,8},{1,13},{5,1},{9,5},{13,9},{2,14},{6,2},{... | collective-permute-start | bytes 688136 | tf_op jit(solution)/shard_map/ppermute | solution.py:19
  12.6 11.5 %collective-permute-start.2 = (bf16[128,896]{1,0:T(8,128)(2,1)S(1)}, bf16[128,896]{1,0:T(8,128)(2,1)S(1)}, u32[]{:S(2)}, u32[]{:S(2)}) collective-permute-start(bf16[128,896]{1,0:T(8,128)(2,1)S(1)} %get-tuple-element.63), channel_id=1, source_target_pairs={{0,8},{4,12},{8,0},{12,4},{1,9},{5,13},{9,1},{13,5},{2,10},{6,14},... | collective-permute-start | bytes 688136 | tf_op jit(solution)/shard_map/ppermute | solution.py:19
  24.1 25.5 %collective-permute-start.3 = (bf16[512,896]{1,0:T(8,128)(2,1)S(1)}, bf16[512,896]{1,0:T(8,128)(2,1)}, u32[]{:S(2)}, u32[]{:S(2)}) collective-permute-start(bf16[512,896]{1,0:T(8,128)(2,1)S(1)} %constant_dynamic-update-slice_fusion), channel_id=1, source_target_pairs={{0,16},{16,32},{32,48},{48,64},{64,80},{80,96},{96,112},{112,0},{1... | collective-permute-start | bytes 2752520 | tf_op jit(solution)/shard_map/ppermute | solution.py:19
  26.1 23.5 %collective-permute-start.5 = (bf16[512,896]{1,0:T(8,128)(2,1)S(1)}, bf16[512,896]{1,0:T(8,128)(2,1)S(1)}, u32[]{:S(2)}, u32[]{:S(2)}) collective-permute-start(bf16[512,896]{1,0:T(8,128)(2,1)S(1)} %constant_dynamic-update-slice_fusion), channel_id=1, source_target_pairs={{0,112},{16,0},{32,16},{48,32},{64,48},{80,64},{96,80},{112,96},{1... | collective-permute-start | bytes 2752520 | tf_op jit(solution)/shard_map/ppermute | solution.py:19
  49.6 22.3 %collective-permute-start.4 = (bf16[512,896]{1,0:T(8,128)(2,1)}, bf16[512,896]{1,0:T(8,128)(2,1)}, u32[]{:S(2)}, u32[]{:S(2)}) collective-permute-start(bf16[512,896]{1,0:T(8,128)(2,1)} %collective-permute-done.3), channel_id=1, source_target_pairs={{0,16},{16,32},{32,48},{48,64},{64,80},{80,96},{96,112},{112,0},{1... | collective-permute-start | bytes 2752520 | tf_op jit(solution)/shard_map/ppermute | solution.py:19
  49.6 4.4 %copy-start.5 = (bf16[512,896]{1,0:T(8,128)(2,1)}, bf16[512,896]{1,0:T(8,128)(2,1)S(1)}, u32[]{:S(2)}) copy-start(bf16[512,896]{1,0:T(8,128)(2,1)S(1)} %collective-permute-done.5) | copy-start | bytes 2752516
  49.6 22.3 %collective-permute-start.6 = (bf16[512,896]{1,0:T(8,128)(2,1)S(1)}, bf16[512,896]{1,0:T(8,128)(2,1)}, u32[]{:S(2)}, u32[]{:S(2)}) collective-permute-start(bf16[512,896]{1,0:T(8,128)(2,1)S(1)} %collective-permute-done.5), channel_id=1, source_target_pairs={{0,112},{16,0},{32,16},{48,32},{64,48},{80,64},{96,80},{112,96},{1... | collective-permute-start | bytes 2752520 | tf_op jit(solution)/shard_map/ppermute | solution.py:19
  54.0 17.9 %all-to-all-start = ((bf16[4,160,896]{2,1,0:T(8,128)(2,1)}), bf16[4,160,896]{2,1,0:T(8,128)(2,1)S(1)}, u32[]{:S(2)}, u32[]{:S(2)}) async-start(bf16[4,160,896]{2,1,0:T(8,128)(2,1)} %pad_maximum_fusion.1), calls=%async_computation | async-start | bytes 2293760 | tf_op jit(solution)/shard_map/all_to_all | solution.py:64
  71.9 1.0 copy-start.3
  72.9 23.5 %collective-permute-start.10 = (bf16[512,896]{1,0:T(8,128)(2,1)}, bf16[512,896]{1,0:T(8,128)(2,1)S(1)}, u32[]{:S(2)}, u32[]{:S(2)}) collective-permute-start(bf16[512,896]{1,0:T(8,128)(2,1)} %collective-permute-done.6), channel_id=1, source_target_pairs={{0,112},{16,0},{32,16},{48,32},{64,48},{80,64},{96,80},{112,96},{1... | collective-permute-start | bytes 2752520 | tf_op jit(solution)/shard_map/ppermute | solution.py:19
  74.5 24.7 %collective-permute-start.9 = (bf16[512,896]{1,0:T(8,128)(2,1)}, bf16[512,896]{1,0:T(8,128)(2,1)S(1)}, u32[]{:S(2)}, u32[]{:S(2)}) collective-permute-start(bf16[512,896]{1,0:T(8,128)(2,1)} %collective-permute-done.4), channel_id=1, source_target_pairs={{0,16},{16,32},{32,48},{48,64},{64,80},{80,96},{96,112},{112,0},{1... | collective-permute-start | bytes 2752520 | tf_op jit(solution)/shard_map/ppermute | solution.py:19
  74.9 3.2 %copy-start.4 = (bf16[4,160,896]{2,1,0:T(8,128)(2,1)S(1)}, bf16[4,160,896]{2,1,0:T(8,128)(2,1)}, u32[]{:S(2)}) copy-start(bf16[4,160,896]{2,1,0:T(8,128)(2,1)} %copy-done.3) | copy-start | bytes 3440644
  79.2 25.7 %collective-permute-start.7 = (bf16[256,896]{1,0:T(8,128)(2,1)S(1)}, bf16[256,896]{1,0:T(8,128)(2,1)S(1)}, u32[]{:S(2)}, u32[]{:S(2)}) collective-permute-start(bf16[256,896]{1,0:T(8,128)(2,1)S(1)} %get-tuple-element.62), channel_id=1, source_target_pairs={{0,16},{16,32},{32,48},{48,64},{64,80},{80,96},{96,112},{112,0},{1... | collective-permute-start | bytes 1376264 | tf_op jit(solution)/shard_map/ppermute | solution.py:19
  79.2 25.6 %collective-permute-start.8 = (bf16[256,896]{1,0:T(8,128)(2,1)S(1)}, bf16[256,896]{1,0:T(8,128)(2,1)S(1)}, u32[]{:S(2)}, u32[]{:S(2)}) collective-permute-start(bf16[256,896]{1,0:T(8,128)(2,1)S(1)} %get-tuple-element.61), channel_id=1, source_target_pairs={{0,112},{16,0},{32,16},{48,32},{64,48},{80,64},{96,80},{112,96},{1... | collective-permute-start | bytes 1376264 | tf_op jit(solution)/shard_map/ppermute | solution.py:19
  89.3 1.2 copy-start.6
  105.9 29.8 %collective-permute-start.12 = (bf16[512,896]{1,0:T(8,128)(2,1)S(1)}, bf16[512,896]{1,0:T(8,128)(2,1)S(1)}, u32[]{:S(2)}, u32[]{:S(2)}) collective-permute-start(bf16[512,896]{1,0:T(8,128)(2,1)S(1)} %pad_maximum_fusion.4), channel_id=1, source_target_pairs={{0,112},{16,0},{32,16},{48,32},{64,48},{80,64},{96,80},{112,96},{1... | collective-permute-start | bytes 2752520 | tf_op jit(solution)/shard_map/ppermute | solution.py:19
  106.4 29.3 %collective-permute-start.11 = (bf16[512,896]{1,0:T(8,128)(2,1)S(1)}, bf16[512,896]{1,0:T(8,128)(2,1)S(1)}, u32[]{:S(2)}, u32[]{:S(2)}) collective-permute-start(bf16[512,896]{1,0:T(8,128)(2,1)S(1)} %pad_maximum_fusion.3), channel_id=1, source_target_pairs={{0,16},{16,32},{32,48},{48,64},{64,80},{80,96},{96,112},{112,0},{1... | collective-permute-start | bytes 2752520 | tf_op jit(solution)/shard_map/ppermute | solution.py:19
  108.2 27.5 %collective-permute-start.13 = (bf16[256,896]{1,0:T(8,128)(2,1)S(1)}, bf16[256,896]{1,0:T(8,128)(2,1)S(1)}, u32[]{:S(2)}, u32[]{:S(2)}) collective-permute-start(bf16[256,896]{1,0:T(8,128)(2,1)S(1)} %slice.84), channel_id=1, source_target_pairs={{0,16},{16,32},{32,48},{48,64},{64,80},{80,96},{96,112},{112,0},{1... | collective-permute-start | bytes 1376264 | tf_op jit(solution)/shard_map/ppermute | solution.py:19
  108.4 27.3 %collective-permute-start.14 = (bf16[256,896]{1,0:T(8,128)(2,1)S(1)}, bf16[256,896]{1,0:T(8,128)(2,1)S(1)}, u32[]{:S(2)}, u32[]{:S(2)}) collective-permute-start(bf16[256,896]{1,0:T(8,128)(2,1)S(1)} %slice.85), channel_id=1, source_target_pairs={{0,112},{16,0},{32,16},{48,32},{64,48},{80,64},{96,80},{112,96},{1... | collective-permute-start | bytes 1376264 | tf_op jit(solution)/shard_map/ppermute | solution.py:19
  136.7 19.1 %collective-permute-start.16 = (bf16[512,896]{1,0:T(8,128)(2,1)S(1)}, bf16[512,896]{1,0:T(8,128)(2,1)S(1)}, u32[]{:S(2)}, u32[]{:S(2)}) collective-permute-start(bf16[512,896]{1,0:T(8,128)(2,1)S(1)} %add_convert_fusion.2), channel_id=1, source_target_pairs={{0,112},{16,0},{32,16},{48,32},{64,48},{80,64},{96,80},{112,96},{1... | collective-permute-start | bytes 2752520 | tf_op jit(solution)/shard_map/ppermute | solution.py:19
  137.8 19.6 %collective-permute-start.15 = (bf16[512,896]{1,0:T(8,128)(2,1)S(1)}, bf16[512,896]{1,0:T(8,128)(2,1)S(1)}, u32[]{:S(2)}, u32[]{:S(2)}) collective-permute-start(bf16[512,896]{1,0:T(8,128)(2,1)S(1)} %add_convert_fusion.3), channel_id=1, source_target_pairs={{0,16},{16,32},{32,48},{48,64},{64,80},{80,96},{96,112},{112,0},{1... | collective-permute-start | bytes 2752520 | tf_op jit(solution)/shard_map/ppermute | solution.py:19
  158.4 17.8 %collective-permute-start.17 = (bf16[512,896]{1,0:T(8,128)(2,1)S(1)}, bf16[512,896]{1,0:T(8,128)(2,1)S(1)}, u32[]{:S(2)}, u32[]{:S(2)}) collective-permute-start(bf16[512,896]{1,0:T(8,128)(2,1)S(1)} %add_convert_fusion.1), channel_id=1, source_target_pairs={{0,16},{16,32},{32,48},{48,64},{64,80},{80,96},{96,112},{112,0},{1... | collective-permute-start | bytes 2752520 | tf_op jit(solution)/shard_map/ppermute | solution.py:19
  161.4 14.8 %collective-permute-start.18 = (bf16[512,896]{1,0:T(8,128)(2,1)S(1)}, bf16[512,896]{1,0:T(8,128)(2,1)S(1)}, u32[]{:S(2)}, u32[]{:S(2)}) collective-permute-start(bf16[512,896]{1,0:T(8,128)(2,1)S(1)} %add_convert_fusion), channel_id=1, source_target_pairs={{0,112},{16,0},{32,16},{48,32},{64,48},{80,64},{96,80},{112,96},{1... | collective-permute-start | bytes 2752520 | tf_op jit(solution)/shard_map/ppermute | solution.py:19
  178.1 21.4 %all-to-all-start.2 = ((bf16[8,128,896]{2,1,0:T(8,128)(2,1)}), bf16[8,128,896]{2,1,0:T(8,128)(2,1)S(1)}, u32[]{:S(2)}, u32[]{:S(2)}) async-start(bf16[8,128,896]{2,1,0:T(8,128)(2,1)} %bitcast.85), calls=%async_computation.2 | async-start | bytes 3670016 | tf_op jit(solution)/shard_map/all_to_all | solution.py:112
  199.5 1.5 copy-start
  199.5 2.0 copy-start.1
Sparse Core Ops, SparseCore 0:
  9.8 44.4 all-gather.2
where the time goes:
time: 212 us; the launch traced here: 211 us
  waiting for transfers between devices  105 us (50%)
  starting transfers between devices  39.7 us (19%)
  matrix products  18.3 us (9%)
  between operations  14.7 us (7%)
  blocking collectives  14.6 us (7%)
  local copies, waits for them, and re-layouts  11.3 us (5%)
  other arithmetic  7.44 us (4%)
    ppermute x19, waiting for transfers between devices, shift(): return lax.ppermute(x, axis, [(i, (i + by) % n) for i in range(n)])  76.3 us
    ppermute x19, starting transfers between devices, shift(): return lax.ppermute(x, axis, [(i, (i + by) % n) for i in range(n)])  31.2 us
    all_to_all x1, blocking collectives, local(): back = lax.all_to_all(grad_h.reshape(Y, toks, part), 'y', 0, 0, tiled=True)  14.6 us
    all_to_all x1, waiting for transfers between devices, local(): got = lax.all_to_all(sent, ('cuts', 'y'), 0, 0, tiled=True)  14.1 us
    all_to_all x1, waiting for transfers between devices, local(): lax.all_to_all(h_sent, 'y', 0, 0, tiled=True).reshape(Y * toks, part)  13.9 us
    dot_general x8, matrix products, product(): return jnp.dot(features(k), w_block, preferred_element_type=f32)  10.5 us
    dot_general x8, matrix products, term(): lax.dot_general(features(k), h_mine, (((0,), (0,)), ((), ())), preferred_...  7.86 us
    all_to_all x1, starting transfers between devices, local(): got = lax.all_to_all(sent, ('cuts', 'y'), 0, 0, tiled=True)  4.92 us
  transfers between devices with their start and end apart: 22, of which 12 were waited for; matrix products, arithmetic and copies ran while one was open for 12% of the time, Pallas kernels for 0%

commit v1 on v0

--- a/solution.py
+++ b/solution.py
@@ -63,13 +63,15 @@
     h_sent = jnp.stack([hidden[:, k * part : (k + 1) * part] for k in range(Y)])
     h_mine = lax.all_to_all(h_sent, "y", 0, 0, tiled=True).reshape(Y * toks, part)
 
-    ups, downs = [w_mine], [w_mine]
+    spans = ((0, 512), (512, part))
+    ups = [[w_mine[:, a:b] for a, b in spans]]
+    downs = [ups[0]]
     for k in (1, 2):
-        ups.append(shift(ups[-1], "z", 1))
-        downs.append(shift(downs[-1], "z", -1))
+        ups.append([shift(x, "z", 1) for x in ups[-1]])
+        downs.append([shift(x, "z", -1) for x in downs[-1]])
     ups[2], downs[2], h_mine = tie((ups[2], downs[2], h_mine))
-    ups.append(shift(ups[2], "z", 1))
-    downs.append(shift(downs[2], "z", -1))
+    ups.append([shift(x, "z", 1) for x in ups[2]])
+    downs.append([shift(x, "z", -1) for x in downs[2]])
 
     def term(k):
         return factor * lax.dot_general(
@@ -87,16 +89,22 @@
     b = term(z - 3)
     down = jnp.concatenate([b[:half], b[half:] + down.astype(f32)], axis=0)
     up, down = shift(up.astype(bf16), "z", 1), shift(down.astype(bf16), "z", -1)
-    last = [shift(ups[3][:half], "z", 1), shift(downs[3][half:], "z", -1)]
-    total = product(z, w_mine)
-    for k in (1, 2, 3):
-        total = total + product(z - k, ups[k]) + product(z + k, downs[k])
+    last = [
+        shift(jnp.concatenate([x[:half] for x in ups[3]], axis=1), "z", 1),
+        shift(jnp.concatenate([x[half:] for x in downs[3]], axis=1), "z", -1),
+    ]
+    total = []
+    for p in range(2):
+        summed = product(z, ups[0][p])
+        for k in (1, 2, 3):
+            summed = summed + product(z - k, ups[k][p]) + product(z + k, downs[k][p])
+        total.append(summed)
     up, down, total, last = tie((up, down, total, last))
     up = (term(z + 2) + up.astype(f32)).astype(bf16)
     down = (term(z - 2) + down.astype(f32)).astype(bf16)
     up, down = shift(up, "z", 1), shift(down, "z", -1)
 
-    total = total + product(z + 4, jnp.concatenate(last, axis=0))
+    total = jnp.concatenate(total, axis=1) + product(z + 4, jnp.concatenate(last, axis=0))
     grad_h = (factor * total).astype(bf16)
     back = lax.all_to_all(grad_h.reshape(Y, toks, part), "y", 0, 0, tiled=True)
     up, down, back = tie((up, down, back))

time: 212 us -> 211 us (level)
  waiting for transfers between devices: 105 us -> 89.9 us
  starting transfers between devices: 39.7 us -> 49.5 us
  matrix products: 18.3 us -> 22.1 us
    ppermute x19 -> x25, starting transfers between devices: 31.2 us -> 41 us  [shift(): return lax.ppermute(x, axis, [(i, (i + by) % n) for i in range(n)])]
    ppermute x19 -> x25, waiting for transfers between devices: 76.3 us -> 68.3 us  [shift(): return lax.ppermute(x, axis, [(i, (i + by) % n) for i in range(n)])]
    all_to_all x1, waiting for transfers between devices: 13.9 us -> 9.02 us  [local(): lax.all_to_all(h_sent, 'y', 0, 0, tiled=True).reshape(Y * toks, part)]
    dot_general x8 -> x15, matrix products: 10.5 us -> 14.2 us  [product(): return jnp.dot(features(k), w_block, preferred_element_type=f32)]
  transfers between devices with their start and end apart: 22 -> 28, of which waited for: 12 -> 19; matrix products, arithmetic and copies ran while one was open for 12% -> 14% of each run, Pallas kernels for 0% -> 0%
where the time goes in v1:
time: 211 us; the launch traced here: 209 us
  waiting for transfers between devices  89.9 us (43%)
  starting transfers between devices  49.5 us (23%)
  matrix products  22.1 us (10%)
  blocking collectives  14.6 us (7%)
  between operations  14.5 us (7%)
  local copies, waits for them, and re-layouts  11.7 us (6%)
  other arithmetic  7.22 us (3%)
    ppermute x25, waiting for transfers between devices, shift(): return lax.ppermute(x, axis, [(i, (i + by) % n) for i in range(n)])  68.3 us
    ppermute x25, starting transfers between devices, shift(): return lax.ppermute(x, axis, [(i, (i + by) % n) for i in range(n)])  41 us
    all_to_all x1, blocking collectives, local(): back = lax.all_to_all(grad_h.reshape(Y, toks, part), 'y', 0, 0, tiled=True)  14.6 us
    dot_general x15, matrix products, product(): return jnp.dot(features(k), w_block, preferred_element_type=f32)  14.2 us
    all_to_all x1, waiting for transfers between devices, local(): got = lax.all_to_all(sent, ('cuts', 'y'), 0, 0, tiled=True)  12 us
    all_to_all x1, waiting for transfers between devices, local(): lax.all_to_all(h_sent, 'y', 0, 0, tiled=True).reshape(Y * toks, part)  9.02 us
    dot_general x8, matrix products, term(): lax.dot_general(features(k), h_mine, (((0,), (0,)), ((), ())), preferred_...  7.87 us
    all_to_all x1, starting transfers between devices, local(): got = lax.all_to_all(sent, ('cuts', 'y'), 0, 0, tiled=True)  4.92 us
  transfers between devices with their start and end apart: 28, of which 19 were waited for; matrix products, arithmetic and copies ran while one was open for 14% of the time, Pallas kernels for 0%

profile of v1, /device:TPU:6, one launch (start us, length us, event | category | flops | bytes accessed | tf_op | source)
XLA Modules:
  0.0 209.5 jit_solution(17208589946560036551)
XLA Ops:
  7.9 1.2 dynamic-slice_bitcast_fusion.8
  9.2 1.7 collective-permute-start
  10.8 1.7 collective-permute-start.1
  12.5 2.0 collective-permute-start.2
  15.6 2.3 %collective-permute-done = bf16[128,896]{1,0:T(8,128)(2,1)S(1)} collective-permute-done((bf16[128,896]{1,0:T(8,128)(2,1)S(1)}, bf16[128,896]{1,0:T(8,128)(2,1)S(1)}, u32[]{:S(2)}, u32[]{:S(2)}) %collective-permute-start) | collective-permute-done | bytes 229408 | tf_op jit(solution)/shard_map/ppermute | solution.py:19
  17.9 4.3 %collective-permute-done.1 = bf16[128,896]{1,0:T(8,128)(2,1)S(1)} collective-permute-done((bf16[128,896]{1,0:T(8,128)(2,1)S(1)}, bf16[128,896]{1,0:T(8,128)(2,1)S(1)}, u32[]{:S(2)}, u32[]{:S(2)}) %collective-permute-start.1) | collective-permute-done | bytes 229408 | tf_op jit(solution)/shard_map/ppermute | solution.py:19
  22.2 1.8 collective-permute-done.2
  24.8 1.9 collective-permute-start.3
  26.7 3.9 %collective-permute-start.7 = (bf16[512,512]{1,0:T(8,128)(2,1)}, bf16[512,512]{1,0:T(8,128)(2,1)S(1)}, u32[]{:S(2)}, u32[]{:S(2)}) collective-permute-start(bf16[512,512]{1,0:T(8,128)(2,1)} %slice.114), channel_id=1, source_target_pairs={{0,112},{16,0},{32,16},{48,32},{64,48},{80,64},{96,80},{112,96},{1... | collective-permute-start | bytes 1572872 | tf_op jit(solution)/shard_map/ppermute | solution.py:19
  30.8 1.2 pad_maximum_fusion.1
  32.0 3.5 %all-to-all-start = ((bf16[4,160,896]{2,1,0:T(8,128)(2,1)}), bf16[4,160,896]{2,1,0:T(8,128)(2,1)S(1)}, u32[]{:S(2)}, u32[]{:S(2)}) async-start(bf16[4,160,896]{2,1,0:T(8,128)(2,1)} %pad_maximum_fusion.1), calls=%async_computation | async-start | bytes 2293760 | tf_op jit(solution)/shard_map/all_to_all | solution.py:64
  35.6 2.1 collective-permute-start.9
  37.7 6.1 %collective-permute-done.3 = bf16[512,512]{1,0:T(8,128)(2,1)S(1)} collective-permute-done((bf16[512,512]{1,0:T(8,128)(2,1)}, bf16[512,512]{1,0:T(8,128)(2,1)S(1)}, u32[]{:S(2)}, u32[]{:S(2)}) %collective-permute-start.3) | collective-permute-done | bytes 524320 | tf_op jit(solution)/shard_map/ppermute | solution.py:19
  43.7 3.2 %collective-permute-start.8 = (bf16[512,512]{1,0:T(8,128)(2,1)S(1)}, bf16[512,512]{1,0:T(8,128)(2,1)}, u32[]{:S(2)}, u32[]{:S(2)}) collective-permute-start(bf16[512,512]{1,0:T(8,128)(2,1)S(1)} %collective-permute-done.7), channel_id=1, source_target_pairs={{0,112},{16,0},{32,16},{48,32},{64,48},{80,64},{96,80},{112,96},{1... | collective-permute-start | bytes 1572872 | tf_op jit(solution)/shard_map/ppermute | solution.py:19
  47.0 4.7 %collective-permute-done.9 = bf16[512,384]{1,0:T(8,128)(2,1)} collective-permute-done((bf16[512,384]{1,0:T(8,128)(2,1)S(1)}, bf16[512,384]{1,0:T(8,128)(2,1)}, u32[]{:S(2)}, u32[]{:S(2)}) %collective-permute-start.9) | collective-permute-done | bytes 393248 | tf_op jit(solution)/shard_map/ppermute | solution.py:19
  51.7 3.8 %collective-permute-start.10 = (bf16[512,384]{1,0:T(8,128)(2,1)}, bf16[512,384]{1,0:T(8,128)(2,1)}, u32[]{:S(2)}, u32[]{:S(2)}) collective-permute-start(bf16[512,384]{1,0:T(8,128)(2,1)} %collective-permute-done.9), channel_id=1, source_target_pairs={{0,112},{16,0},{32,16},{48,32},{64,48},{80,64},{96,80},{112,96},{1... | collective-permute-start | bytes 1179656 | tf_op jit(solution)/shard_map/ppermute | solution.py:19
  55.5 9.0 %all-to-all-done = bf16[4,160,896]{2,1,0:T(8,128)(2,1)S(1)} async-done(((bf16[4,160,896]{2,1,0:T(8,128)(2,1)}), bf16[4,160,896]{2,1,0:T(8,128)(2,1)S(1)}, u32[]{:S(2)}, u32[]{:S(2)}) %all-to-all-start) | async-done | bytes 1146912 | tf_op jit(solution)/shard_map/all_to_all | solution.py:64
  64.5 4.9 %collective-permute-done.10 = bf16[512,384]{1,0:T(8,128)(2,1)} collective-permute-done((bf16[512,384]{1,0:T(8,128)(2,1)}, bf16[512,384]{1,0:T(8,128)(2,1)}, u32[]{:S(2)}, u32[]{:S(2)}) %collective-permute-start.10) | collective-permute-done | bytes 393248 | tf_op jit(solution)/shard_map/ppermute | solution.py:19
  70.8 3.1 %collective-permute-start.15 = (bf16[512,512]{1,0:T(8,128)(2,1)}, bf16[512,512]{1,0:T(8,128)(2,1)S(1)}, u32[]{:S(2)}, u32[]{:S(2)}) collective-permute-start(bf16[512,512]{1,0:T(8,128)(2,1)} %collective-permute-done.8), channel_id=1, source_target_pairs={{0,112},{16,0},{32,16},{48,32},{64,48},{80,64},{96,80},{112,96},{1... | collective-permute-start | bytes 1572872 | tf_op jit(solution)/shard_map/ppermute | solution.py:19
  73.8 3.2 %collective-permute-start.16 = (bf16[512,384]{1,0:T(8,128)(2,1)}, bf16[512,384]{1,0:T(8,128)(2,1)}, u32[]{:S(2)}, u32[]{:S(2)}) collective-permute-start(bf16[512,384]{1,0:T(8,128)(2,1)} %collective-permute-done.10), channel_id=1, source_target_pairs={{0,112},{16,0},{32,16},{48,32},{64,48},{80,64},{96,80},{112,96},{1... | collective-permute-start | bytes 1179656 | tf_op jit(solution)/shard_map/ppermute | solution.py:19
  77.1 3.1 %constant_dynamic-slice_fusion = (bf16[4,1,160,512]{3,2,1,0:T(8,128)(2,1)S(1)}, bf16[4,1,160,512]{3,2,1,0:T(8,128)(2,1)S(1)}, bf16[4,1,160,512]{3,2,1,0:T(8,128)...) fusion(bf16[4,4,160,1024]{3,2,1,0:T(8,128)(2,1)} %bitcast.119, ...), kind=kLoop, calls=%fused_computation.71 | loop fusion | bytes 10485824 | tf_op jit(solution)/shard_map/dynamic_slice | solution.py:51
  81.3 1.5 fusion.28
  84.9 1.6 fusion.31
  87.5 1.5 fusion.32
  89.5 5.3 %collective-permute-done.14 = bf16[512,384]{1,0:T(8,128)(2,1)S(1)} collective-permute-done((bf16[512,384]{1,0:T(8,128)(2,1)}, bf16[512,384]{1,0:T(8,128)(2,1)S(1)}, u32[]{:S(2)}, u32[]{:S(2)}) %collective-permute-start.14) | collective-permute-done | bytes 393248 | tf_op jit(solution)/shard_map/ppermute | solution.py:19
  94.8 1.9 collective-permute-start.12
  96.7 1.5 fusion.33
  98.9 3.1 %collective-permute-done.11 = bf16[256,896]{1,0:T(8,128)(2,1)S(1)} collective-permute-done((bf16[256,896]{1,0:T(8,128)(2,1)S(1)}, bf16[256,896]{1,0:T(8,128)(2,1)S(1)}, u32[]{:S(2)}, u32[]{:S(2)}) %collective-permute-start.11) | collective-permute-done | bytes 458784 | tf_op jit(solution)/shard_map/ppermute | solution.py:19
  102.0 1.4 collective-permute-done.12
  104.8 1.5 fusion.35
  106.4 3.1 %collective-permute-start.20 = (bf16[256,896]{1,0:T(8,128)(2,1)S(1)}, bf16[256,896]{1,0:T(8,128)(2,1)S(1)}, u32[]{:S(2)}, u32[]{:S(2)}) collective-permute-start(bf16[256,896]{1,0:T(8,128)(2,1)S(1)} %pad_maximum_fusion.7), channel_id=1, source_target_pairs={{0,112},{16,0},{32,16},{48,32},{64,48},{80,64},{96,80},{112,96},{1... | collective-permute-start | bytes 1376264 | tf_op jit(solution)/shard_map/ppermute | solution.py:19
  109.9 3.3 %collective-permute-start.18 = (bf16[512,896]{1,0:T(8,128)(2,1)S(1)}, bf16[512,896]{1,0:T(8,128)(2,1)S(1)}, u32[]{:S(2)}, u32[]{:S(2)}) collective-permute-start(bf16[512,896]{1,0:T(8,128)(2,1)S(1)} %pad_maximum_fusion.4), channel_id=1, source_target_pairs={{0,112},{16,0},{32,16},{48,32},{64,48},{80,64},{96,80},{112,96},{1... | collective-permute-start | bytes 2752520 | tf_op jit(solution)/shard_map/ppermute | solution.py:19
  115.3 1.6 fusion.7
  116.9 3.7 %collective-permute-done.20 = bf16[256,896]{1,0:T(8,128)(2,1)S(1)} collective-permute-done((bf16[256,896]{1,0:T(8,128)(2,1)S(1)}, bf16[256,896]{1,0:T(8,128)(2,1)S(1)}, u32[]{:S(2)}, u32[]{:S(2)}) %collective-permute-start.20) | collective-permute-done | bytes 458784 | tf_op jit(solution)/shard_map/ppermute | solution.py:19
  120.5 3.8 %collective-permute-done.19 = bf16[256,896]{1,0:T(8,128)(2,1)S(1)} collective-permute-done((bf16[256,896]{1,0:T(8,128)(2,1)S(1)}, bf16[256,896]{1,0:T(8,128)(2,1)S(1)}, u32[]{:S(2)}, u32[]{:S(2)}) %collective-permute-start.19) | collective-permute-done | bytes 458784 | tf_op jit(solution)/shard_map/ppermute | solution.py:19
  124.4 11.0 %collective-permute-done.18 = bf16[512,896]{1,0:T(8,128)(2,1)S(1)} collective-permute-done((bf16[512,896]{1,0:T(8,128)(2,1)S(1)}, bf16[512,896]{1,0:T(8,128)(2,1)S(1)}, u32[]{:S(2)}, u32[]{:S(2)}) %collective-permute-start.18) | collective-permute-done | bytes 917536 | tf_op jit(solution)/shard_map/ppermute | solution.py:19
  135.4 2.4 %collective-permute-done.17 = bf16[512,896]{1,0:T(8,128)(2,1)S(1)} collective-permute-done((bf16[512,896]{1,0:T(8,128)(2,1)S(1)}, bf16[512,896]{1,0:T(8,128)(2,1)S(1)}, u32[]{:S(2)}, u32[]{:S(2)}) %collective-permute-start.17) | collective-permute-done | bytes 917536 | tf_op jit(solution)/shard_map/ppermute | solution.py:19
  138.8 1.1 collective-permute-start.22
  142.8 14.6 %all_to_all.15 = bf16[4,160,896]{2,1,0:T(8,128)(2,1)} all-to-all(bf16[4,160,896]{2,1,0:T(8,128)(2,1)S(1)} %bitcast.128), channel_id=1, replica_groups=mesh['cuts'=2,'z'=8,'y'=4,'xl'=2,'core'=2] {'y'}, dimensions={0} | all-to-all | bytes 2293760 | tf_op jit(solution)/shard_map/all_to_all | solution.py:109
  157.4 3.0 %collective-permute-done.21 = bf16[512,896]{1,0:T(8,128)(2,1)S(1)} collective-permute-done((bf16[512,896]{1,0:T(8,128)(2,1)S(1)}, bf16[512,896]{1,0:T(8,128)(2,1)S(1)}, u32[]{:S(2)}, u32[]{:S(2)}) %collective-permute-start.21) | collective-permute-done | bytes 917536 | tf_op jit(solution)/shard_map/ppermute | solution.py:19
  162.5 3.3 %collective-permute-start.24 = (bf16[512,896]{1,0:T(8,128)(2,1)S(1)}, bf16[512,896]{1,0:T(8,128)(2,1)S(1)}, u32[]{:S(2)}, u32[]{:S(2)}) collective-permute-start(bf16[512,896]{1,0:T(8,128)(2,1)S(1)} %add_convert_fusion), channel_id=1, source_target_pairs={{0,112},{16,0},{32,16},{48,32},{64,48},{80,64},{96,80},{112,96},{1... | collective-permute-start | bytes 2752520 | tf_op jit(solution)/shard_map/ppermute | solution.py:19
  166.8 9.6 %collective-permute-done.23 = bf16[512,896]{1,0:T(8,128)(2,1)S(1)} collective-permute-done((bf16[512,896]{1,0:T(8,128)(2,1)S(1)}, bf16[512,896]{1,0:T(8,128)(2,1)S(1)}, u32[]{:S(2)}, u32[]{:S(2)}) %collective-permute-start.23) | collective-permute-done | bytes 917536 | tf_op jit(solution)/shard_map/ppermute | solution.py:19
  177.2 1.4 pad_maximum_fusion
  178.6 4.9 %all-to-all-start.2 = ((bf16[8,128,896]{2,1,0:T(8,128)(2,1)}), bf16[8,128,896]{2,1,0:T(8,128)(2,1)S(1)}, u32[]{:S(2)}, u32[]{:S(2)}) async-start(bf16[8,128,896]{2,1,0:T(8,128)(2,1)} %bitcast.97), calls=%async_computation.2 | async-start | bytes 3670016 | tf_op jit(solution)/shard_map/all_to_all | solution.py:120
  183.5 1.3 slice_bitcast_fusion.3
  185.9 12.0 %all-to-all-done.2 = bf16[8,128,896]{2,1,0:T(8,128)(2,1)S(1)} async-done(((bf16[8,128,896]{2,1,0:T(8,128)(2,1)}), bf16[8,128,896]{2,1,0:T(8,128)(2,1)S(1)}, u32[]{:S(2)}, u32[]{:S(2)}) %all-to-all-start.2) | async-done | bytes 1835040 | tf_op jit(solution)/shard_map/all_to_all | solution.py:120
  198.1 1.3 copy-done
  199.9 2.7 %fusion.13 = (bf16[1,128,3584]{2,1,0:T(8,128)(2,1)}, f32[128,3584]{1,0:T(8,128)}, f32[128,3584]{1,0:T(8,128)}) fusion(bf16[128,896]{1,0:T(8,128)(2,1)S(1)} %get-tuple-element.62, bf16[128,896]{1,0:T(8,128)(2,1)S(1)} %get-tuple-element.58, bf16[128,896]{1,0:T(8,128)(2,1)S(1)} %get-tuple-element.59, bf16[128,896]{1,0:T(8,128)(2,1)S(1)} %get-tuple-element.60, ...), kind=kLoop, calls=%fused_computation.35 | loop fusion | flops 15138816 | bytes 10092544 | tf_op jit(solution)/shard_map/broadcast_in_dim | solution.py:137
  (84 shorter events, 23.0 us)
Async XLA Ops:
  7.2 69.9 %all-gather.3.cloned.1.call-start = ((), (), s32[]{:S(2)}) async-start(), calls=%async_computation.3 | async-start | bytes 5570560 | tf_op jit(solution)/shard_map/all_gather | solution.py:45
  9.2 8.7 %collective-permute-start = (bf16[128,896]{1,0:T(8,128)(2,1)S(1)}, bf16[128,896]{1,0:T(8,128)(2,1)S(1)}, u32[]{:S(2)}, u32[]{:S(2)}) collective-permute-start(bf16[128,896]{1,0:T(8,128)(2,1)S(1)} %get-tuple-element.74), channel_id=1, source_target_pairs={{0,4},{4,8},{8,12},{12,0},{1,5},{5,9},{9,13},{13,1},{2,6},{6,10},{... | collective-permute-start | bytes 688136 | tf_op jit(solution)/shard_map/ppermute | solution.py:19
  10.8 11.3 %collective-permute-start.1 = (bf16[128,896]{1,0:T(8,128)(2,1)S(1)}, bf16[128,896]{1,0:T(8,128)(2,1)S(1)}, u32[]{:S(2)}, u32[]{:S(2)}) collective-permute-start(bf16[128,896]{1,0:T(8,128)(2,1)S(1)} %get-tuple-element.75), channel_id=1, source_target_pairs={{0,12},{4,0},{8,4},{12,8},{1,13},{5,1},{9,5},{13,9},{2,14},{6,2},{... | collective-permute-start | bytes 688136 | tf_op jit(solution)/shard_map/ppermute | solution.py:19
  12.5 11.5 %collective-permute-start.2 = (bf16[128,896]{1,0:T(8,128)(2,1)S(1)}, bf16[128,896]{1,0:T(8,128)(2,1)S(1)}, u32[]{:S(2)}, u32[]{:S(2)}) collective-permute-start(bf16[128,896]{1,0:T(8,128)(2,1)S(1)} %get-tuple-element.73), channel_id=1, source_target_pairs={{0,8},{4,12},{8,0},{12,4},{1,9},{5,13},{9,1},{13,5},{2,10},{6,14},... | collective-permute-start | bytes 688136 | tf_op jit(solution)/shard_map/ppermute | solution.py:19
  14.5 16.2 %copy-start.2 = (bf16[160,3584]{1,0:T(8,128)(2,1)S(1)}, bf16[160,3584]{1,0:T(8,128)(2,1)}, u32[]{:S(2)}) copy-start(bf16[160,3584]{1,0:T(8,128)(2,1)} %param.5) | copy-start | bytes 3440644
  24.8 18.9 %collective-permute-start.3 = (bf16[512,512]{1,0:T(8,128)(2,1)}, bf16[512,512]{1,0:T(8,128)(2,1)S(1)}, u32[]{:S(2)}, u32[]{:S(2)}) collective-permute-start(bf16[512,512]{1,0:T(8,128)(2,1)} %slice.114), channel_id=1, source_target_pairs={{0,16},{16,32},{32,48},{48,64},{64,80},{80,96},{96,112},{112,0},{1... | collective-permute-start | bytes 1572872 | tf_op jit(solution)/shard_map/ppermute | solution.py:19
  26.7 17.0 %collective-permute-start.7 = (bf16[512,512]{1,0:T(8,128)(2,1)}, bf16[512,512]{1,0:T(8,128)(2,1)S(1)}, u32[]{:S(2)}, u32[]{:S(2)}) collective-permute-start(bf16[512,512]{1,0:T(8,128)(2,1)} %slice.114), channel_id=1, source_target_pairs={{0,112},{16,0},{32,16},{48,32},{64,48},{80,64},{96,80},{112,96},{1... | collective-permute-start | bytes 1572872 | tf_op jit(solution)/shard_map/ppermute | solution.py:19
  32.0 32.6 %all-to-all-start = ((bf16[4,160,896]{2,1,0:T(8,128)(2,1)}), bf16[4,160,896]{2,1,0:T(8,128)(2,1)S(1)}, u32[]{:S(2)}, u32[]{:S(2)}) async-start(bf16[4,160,896]{2,1,0:T(8,128)(2,1)} %pad_maximum_fusion.1), calls=%async_computation | async-start | bytes 2293760 | tf_op jit(solution)/shard_map/all_to_all | solution.py:64
  35.6 16.1 %collective-permute-start.9 = (bf16[512,384]{1,0:T(8,128)(2,1)S(1)}, bf16[512,384]{1,0:T(8,128)(2,1)}, u32[]{:S(2)}, u32[]{:S(2)}) collective-permute-start(bf16[512,384]{1,0:T(8,128)(2,1)S(1)} %slice.115), channel_id=1, source_target_pairs={{0,112},{16,0},{32,16},{48,32},{64,48},{80,64},{96,80},{112,96},{1... | collective-permute-start | bytes 1179656 | tf_op jit(solution)/shard_map/ppermute | solution.py:19
  37.6 17.9 %collective-permute-start.5 = (bf16[512,384]{1,0:T(8,128)(2,1)S(1)}, bf16[512,384]{1,0:T(8,128)(2,1)}, u32[]{:S(2)}, u32[]{:S(2)}) collective-permute-start(bf16[512,384]{1,0:T(8,128)(2,1)S(1)} %slice.115), channel_id=1, source_target_pairs={{0,16},{16,32},{32,48},{48,64},{64,80},{80,96},{96,112},{112,0},{1... | collective-permute-start | bytes 1179656 | tf_op jit(solution)/shard_map/ppermute | solution.py:19
  43.7 26.3 %copy-start.4 = (bf16[512,512]{1,0:T(8,128)(2,1)}, bf16[512,512]{1,0:T(8,128)(2,1)S(1)}, u32[]{:S(2)}) copy-start(bf16[512,512]{1,0:T(8,128)(2,1)S(1)} %collective-permute-done.3) | copy-start | bytes 1572868
  43.7 26.3 %collective-permute-start.4 = (bf16[512,512]{1,0:T(8,128)(2,1)S(1)}, bf16[512,512]{1,0:T(8,128)(2,1)}, u32[]{:S(2)}, u32[]{:S(2)}) collective-permute-start(bf16[512,512]{1,0:T(8,128)(2,1)S(1)} %collective-permute-done.3), channel_id=1, source_target_pairs={{0,16},{16,32},{32,48},{48,64},{64,80},{80,96},{96,112},{112,0},{1... | collective-permute-start | bytes 1572872 | tf_op jit(solution)/shard_map/ppermute | solution.py:19
  43.7 26.3 %copy-start.6 = (bf16[512,512]{1,0:T(8,128)(2,1)}, bf16[512,512]{1,0:T(8,128)(2,1)S(1)}, u32[]{:S(2)}) copy-start(bf16[512,512]{1,0:T(8,128)(2,1)S(1)} %collective-permute-done.7) | copy-start | bytes 1572868
  43.7 26.3 %collective-permute-start.8 = (bf16[512,512]{1,0:T(8,128)(2,1)S(1)}, bf16[512,512]{1,0:T(8,128)(2,1)}, u32[]{:S(2)}, u32[]{:S(2)}) collective-permute-start(bf16[512,512]{1,0:T(8,128)(2,1)S(1)} %collective-permute-done.7), channel_id=1, source_target_pairs={{0,112},{16,0},{32,16},{48,32},{64,48},{80,64},{96,80},{112,96},{1... | collective-permute-start | bytes 1572872 | tf_op jit(solution)/shard_map/ppermute | solution.py:19
  51.7 17.7 %collective-permute-start.10 = (bf16[512,384]{1,0:T(8,128)(2,1)}, bf16[512,384]{1,0:T(8,128)(2,1)}, u32[]{:S(2)}, u32[]{:S(2)}) collective-permute-start(bf16[512,384]{1,0:T(8,128)(2,1)} %collective-permute-done.9), channel_id=1, source_target_pairs={{0,112},{16,0},{32,16},{48,32},{64,48},{80,64},{96,80},{112,96},{1... | collective-permute-start | bytes 1179656 | tf_op jit(solution)/shard_map/ppermute | solution.py:19
  55.5 14.5 %collective-permute-start.6 = (bf16[512,384]{1,0:T(8,128)(2,1)}, bf16[512,384]{1,0:T(8,128)(2,1)S(1)}, u32[]{:S(2)}, u32[]{:S(2)}) collective-permute-start(bf16[512,384]{1,0:T(8,128)(2,1)} %collective-permute-done.5), channel_id=1, source_target_pairs={{0,16},{16,32},{32,48},{48,64},{64,80},{80,96},{96,112},{112,0},{1... | collective-permute-start | bytes 1179656 | tf_op jit(solution)/shard_map/ppermute | solution.py:19
  70.0 0.7 copy-start.8
  70.1 28.8 %collective-permute-start.13 = (bf16[512,512]{1,0:T(8,128)(2,1)}, bf16[512,512]{1,0:T(8,128)(2,1)S(1)}, u32[]{:S(2)}, u32[]{:S(2)}) collective-permute-start(bf16[512,512]{1,0:T(8,128)(2,1)} %collective-permute-done.4), channel_id=1, source_target_pairs={{0,16},{16,32},{32,48},{48,64},{64,80},{80,96},{96,112},{112,0},{1... | collective-permute-start | bytes 1572872 | tf_op jit(solution)/shard_map/ppermute | solution.py:19
  70.8 28.1 %collective-permute-start.15 = (bf16[512,512]{1,0:T(8,128)(2,1)}, bf16[512,512]{1,0:T(8,128)(2,1)S(1)}, u32[]{:S(2)}, u32[]{:S(2)}) collective-permute-start(bf16[512,512]{1,0:T(8,128)(2,1)} %collective-permute-done.8), channel_id=1, source_target_pairs={{0,112},{16,0},{32,16},{48,32},{64,48},{80,64},{96,80},{112,96},{1... | collective-permute-start | bytes 1572872 | tf_op jit(solution)/shard_map/ppermute | solution.py:19
  73.8 21.0 %collective-permute-start.14 = (bf16[512,384]{1,0:T(8,128)(2,1)}, bf16[512,384]{1,0:T(8,128)(2,1)S(1)}, u32[]{:S(2)}, u32[]{:S(2)}) collective-permute-start(bf16[512,384]{1,0:T(8,128)(2,1)} %copy-done.8), channel_id=1, source_target_pairs={{0,16},{16,32},{32,48},{48,64},{64,80},{80,96},{96,112},{112,0},{1... | collective-permute-start | bytes 1179656 | tf_op jit(solution)/shard_map/ppermute | solution.py:19
  73.8 25.0 %collective-permute-start.16 = (bf16[512,384]{1,0:T(8,128)(2,1)}, bf16[512,384]{1,0:T(8,128)(2,1)}, u32[]{:S(2)}, u32[]{:S(2)}) collective-permute-start(bf16[512,384]{1,0:T(8,128)(2,1)} %collective-permute-done.10), channel_id=1, source_target_pairs={{0,112},{16,0},{32,16},{48,32},{64,48},{80,64},{96,80},{112,96},{1... | collective-permute-start | bytes 1179656 | tf_op jit(solution)/shard_map/ppermute | solution.py:19
  81.2 20.7 %collective-permute-start.11 = (bf16[256,896]{1,0:T(8,128)(2,1)S(1)}, bf16[256,896]{1,0:T(8,128)(2,1)S(1)}, u32[]{:S(2)}, u32[]{:S(2)}) collective-permute-start(bf16[256,896]{1,0:T(8,128)(2,1)S(1)} %get-tuple-element.72), channel_id=1, source_target_pairs={{0,16},{16,32},{32,48},{48,64},{64,80},{80,96},{96,112},{112,0},{1... | collective-permute-start | bytes 1376264 | tf_op jit(solution)/shard_map/ppermute | solution.py:19
  84.9 1.6 copy-start.5
  84.9 2.1 %copy-start.7 = (bf16[512,512]{1,0:T(8,128)(2,1)S(1)}, bf16[512,512]{1,0:T(8,128)(2,1)}, u32[]{:S(2)}) copy-start(bf16[512,512]{1,0:T(8,128)(2,1)} %copy-done.6) | copy-start | bytes 1572868
  94.8 8.5 %copy-start.3 = (bf16[512,384]{1,0:T(8,128)(2,1)}, bf16[512,384]{1,0:T(8,128)(2,1)S(1)}, u32[]{:S(2)}) copy-start(bf16[512,384]{1,0:T(8,128)(2,1)S(1)} %collective-permute-done.14) | copy-start | bytes 1179652
  94.8 8.5 %collective-permute-start.12 = (bf16[256,896]{1,0:T(8,128)(2,1)S(1)}, bf16[256,896]{1,0:T(8,128)(2,1)S(1)}, u32[]{:S(2)}, u32[]{:S(2)}) collective-permute-start(bf16[256,896]{1,0:T(8,128)(2,1)S(1)} %get-tuple-element.71), channel_id=1, source_target_pairs={{0,112},{16,0},{32,16},{48,32},{64,48},{80,64},{96,80},{112,96},{1... | collective-permute-start | bytes 1376264 | tf_op jit(solution)/shard_map/ppermute | solution.py:19
  104.8 4.8 %slice-start = ((bf16[512,384]{1,0:T(8,128)(2,1)}), bf16[256,384]{1,0:T(8,128)(2,1)S(1)}, s32[]{:S(2)}) async-start(bf16[512,384]{1,0:T(8,128)(2,1)} %copy-done.3), calls=%async_computation.4 | async-start | bytes 393216 | tf_op jit(solution)/shard_map/slice | solution.py:93
  106.4 14.1 %collective-permute-start.20 = (bf16[256,896]{1,0:T(8,128)(2,1)S(1)}, bf16[256,896]{1,0:T(8,128)(2,1)S(1)}, u32[]{:S(2)}, u32[]{:S(2)}) collective-permute-start(bf16[256,896]{1,0:T(8,128)(2,1)S(1)} %pad_maximum_fusion.7), channel_id=1, source_target_pairs={{0,112},{16,0},{32,16},{48,32},{64,48},{80,64},{96,80},{112,96},{1... | collective-permute-start | bytes 1376264 | tf_op jit(solution)/shard_map/ppermute | solution.py:19
  109.6 14.7 %collective-permute-start.19 = (bf16[256,896]{1,0:T(8,128)(2,1)S(1)}, bf16[256,896]{1,0:T(8,128)(2,1)S(1)}, u32[]{:S(2)}, u32[]{:S(2)}) collective-permute-start(bf16[256,896]{1,0:T(8,128)(2,1)S(1)} %pad_maximum_fusion.6), channel_id=1, source_target_pairs={{0,16},{16,32},{32,48},{48,64},{64,80},{80,96},{96,112},{112,0},{1... | collective-permute-start | bytes 1376264 | tf_op jit(solution)/shard_map/ppermute | solution.py:19
  109.9 3.8 %copy-start.9 = (bf16[512,384]{1,0:T(8,128)(2,1)S(1)}, bf16[512,384]{1,0:T(8,128)(2,1)}, u32[]{:S(2)}) copy-start(bf16[512,384]{1,0:T(8,128)(2,1)} %copy-done.8) | copy-start | bytes 1179652
  109.9 25.5 %collective-permute-start.18 = (bf16[512,896]{1,0:T(8,128)(2,1)S(1)}, bf16[512,896]{1,0:T(8,128)(2,1)S(1)}, u32[]{:S(2)}, u32[]{:S(2)}) collective-permute-start(bf16[512,896]{1,0:T(8,128)(2,1)S(1)} %pad_maximum_fusion.4), channel_id=1, source_target_pairs={{0,112},{16,0},{32,16},{48,32},{64,48},{80,64},{96,80},{112,96},{1... | collective-permute-start | bytes 2752520 | tf_op jit(solution)/shard_map/ppermute | solution.py:19
  113.4 24.4 %collective-permute-start.17 = (bf16[512,896]{1,0:T(8,128)(2,1)S(1)}, bf16[512,896]{1,0:T(8,128)(2,1)S(1)}, u32[]{:S(2)}, u32[]{:S(2)}) collective-permute-start(bf16[512,896]{1,0:T(8,128)(2,1)S(1)} %pad_maximum_fusion.3), channel_id=1, source_target_pairs={{0,16},{16,32},{32,48},{48,64},{64,80},{80,96},{96,112},{112,0},{1... | collective-permute-start | bytes 2752520 | tf_op jit(solution)/shard_map/ppermute | solution.py:19
  138.8 18.6 %collective-permute-start.22 = (bf16[512,896]{1,0:T(8,128)(2,1)S(1)}, bf16[512,896]{1,0:T(8,128)(2,1)S(1)}, u32[]{:S(2)}, u32[]{:S(2)}) collective-permute-start(bf16[512,896]{1,0:T(8,128)(2,1)S(1)} %add_convert_fusion.2), channel_id=1, source_target_pairs={{0,112},{16,0},{32,16},{48,32},{64,48},{80,64},{96,80},{112,96},{1... | collective-permute-start | bytes 2752520 | tf_op jit(solution)/shard_map/ppermute | solution.py:19
  140.9 19.5 %collective-permute-start.21 = (bf16[512,896]{1,0:T(8,128)(2,1)S(1)}, bf16[512,896]{1,0:T(8,128)(2,1)S(1)}, u32[]{:S(2)}, u32[]{:S(2)}) collective-permute-start(bf16[512,896]{1,0:T(8,128)(2,1)S(1)} %add_convert_fusion.3), channel_id=1, source_target_pairs={{0,16},{16,32},{32,48},{48,64},{64,80},{80,96},{96,112},{112,0},{1... | collective-permute-start | bytes 2752520 | tf_op jit(solution)/shard_map/ppermute | solution.py:19
  161.4 14.9 %collective-permute-start.23 = (bf16[512,896]{1,0:T(8,128)(2,1)S(1)}, bf16[512,896]{1,0:T(8,128)(2,1)S(1)}, u32[]{:S(2)}, u32[]{:S(2)}) collective-permute-start(bf16[512,896]{1,0:T(8,128)(2,1)S(1)} %add_convert_fusion.1), channel_id=1, source_target_pairs={{0,16},{16,32},{32,48},{48,64},{64,80},{80,96},{96,112},{112,0},{1... | collective-permute-start | bytes 2752520 | tf_op jit(solution)/shard_map/ppermute | solution.py:19
  162.5 14.2 %collective-permute-start.24 = (bf16[512,896]{1,0:T(8,128)(2,1)S(1)}, bf16[512,896]{1,0:T(8,128)(2,1)S(1)}, u32[]{:S(2)}, u32[]{:S(2)}) collective-permute-start(bf16[512,896]{1,0:T(8,128)(2,1)S(1)} %add_convert_fusion), channel_id=1, source_target_pairs={{0,112},{16,0},{32,16},{48,32},{64,48},{80,64},{96,80},{112,96},{1... | collective-permute-start | bytes 2752520 | tf_op jit(solution)/shard_map/ppermute | solution.py:19
  178.6 19.3 %all-to-all-start.2 = ((bf16[8,128,896]{2,1,0:T(8,128)(2,1)}), bf16[8,128,896]{2,1,0:T(8,128)(2,1)S(1)}, u32[]{:S(2)}, u32[]{:S(2)}) async-start(bf16[8,128,896]{2,1,0:T(8,128)(2,1)} %bitcast.97), calls=%async_computation.2 | async-start | bytes 3670016 | tf_op jit(solution)/shard_map/all_to_all | solution.py:120
  197.9 1.5 copy-start
  197.9 2.0 copy-start.1
Sparse Core Ops, SparseCore 0:
  9.8 55.4 all-gather.2
